TPU v7x, 32 devices: a whole 2x2x4 slice. The times are simulated.
32 devices in a mesh: frame: 8 (over z, x), head: 4 (over y, core).
Axes of the slice: x: 2, y: 2, z: 4, core: 2. Of those that a mesh axis runs over, the one named last changes fastest.
Arguments:
- queries: bfloat16 [16, 8, 32, 896], P('frame', None, None, 'head'), may hold values from -6 to 6
- key_vectors: bfloat16 [16, 8, 32, 896], P('frame', None, None, 'head'), may hold values from -6 to 6
- value_vectors: bfloat16 [16, 8, 32, 896], P('frame', None, None, 'head'), may hold values from -8 to 8
- frame_index: int32 [16], P('frame'), may hold values from 0 to 31, as said below
- height_index: int32 [8], replicated, may hold values from 0 to 15, as said below
- width_index: int32 [32], replicated, may hold values from 0 to 63, as said below
- frame_block: int32 [16], P('frame'), may hold values from 0 to 4, never falling along the last dimension, each value on 1 to 6 neighbouring positions
- conv_weight: bfloat16 [3, 896, 2240], P(None, 'head'), may hold values from -0.125 to 0.125
- conv_bias: float32 [2240], replicated, may hold values from -0.8 to 0.8
Outputs:
- mixed_frames: bfloat16 [8, 16, 32, 2240], P('head', 'frame')
Inputs may be any that keep to these rules, and one draw needn't show every extreme that they name: `frame_index`: strictly increasing over the frames, first entry 0, last entry 31. `height_index`: strictly increasing over the rows, first entry 0, last entry 15. `width_index`: strictly increasing over the columns, first entry 0, last entry 63.
All inputs are finite; a program needn't handle non-finite values.
Results may differ from a plain program's by a relative error of at most 0.0043.
The roundings to bfloat16 on the way count: a program that leaves them out, or rounds other values in their place, can miss the bound.
Values may be sent and summed in bfloat16 or wider, within the bound.
A program may use at most 128 MiB of HBM per device.

v0:
```python
import jax
import jax.numpy as jnp
from jax import lax
from jax.sharding import PartitionSpec as P

HD = 112


EPSILON = 1e-06
HIGHEST = lax.Precision.HIGHEST


def prefix(value, axis, join, neutral, backward):
    count, mine = (lax.axis_size(axis), lax.axis_index(axis))
    pieces = jax.tree.map(lambda part: lax.all_gather(part, axis), value)
    if backward:
        pieces = jax.tree.map(lambda part: part[::-1], pieces)
        mine = count - 1 - mine
    so_far = jax.tree.map(
        lambda part, zero: jnp.full_like(part, 0) + jnp.asarray(zero, part.dtype), value, neutral
    )

    def step(position, so_far):
        longer = join(so_far, jax.tree.map(lambda part: part[position], pieces))
        return jax.tree.map(lambda new, old: jnp.where(position < mine, new, old), longer, so_far)

    return lax.fori_loop(0, count - 1, step, so_far)


def shifted(value, axis, by):
    length = lax.axis_size(axis)
    pairs = [(i, i + by) for i in range(length) if 0 <= i + by < length]
    return lax.ppermute(value, axis, pairs)


def spin_part(section, positions, axis_slot):
    half_size = section.shape[-1] // 2
    inverse = 10000.0 ** (-2.0 * jnp.arange(half_size, dtype=jnp.float32) / section.shape[-1])
    angles = positions.astype(jnp.float32)[:, None] * inverse[None, :]
    target = [1, 1, 1, 1, half_size]
    target[axis_slot] = positions.shape[0]
    angles = angles.reshape(target)
    cosine = jnp.cos(angles)
    sine_values = jnp.sin(angles)
    lower_half = section[..., :half_size]
    upper_half = section[..., half_size:]
    return jnp.concatenate(
        [
            lower_half * cosine - upper_half * sine_values,
            upper_half * cosine + lower_half * sine_values,
        ],
        axis=-1,
    )


def rotate(values, frame_pos, height_pos, width_pos):
    head_size = values.shape[-1]
    side_size = head_size * 5 // 14 // 2 * 2
    first_size = head_size - 2 * side_size
    return jnp.concatenate(
        [
            spin_part(values[..., :first_size], frame_pos, 0),
            spin_part(values[..., first_size : first_size + side_size], height_pos, 1),
            spin_part(values[..., first_size + side_size :], width_pos, 2),
        ],
        axis=-1,
    )


def add_pair(earlier, later):
    return (earlier[0] + later[0], earlier[1] + later[1])


def join_tails(earlier, later):
    high_id, high_state, high_sum = earlier
    low_id, low_state, low_sum = later
    vacant = low_id < 0.0
    same_block = high_id == low_id
    joined_id = jnp.where(vacant, high_id, low_id)
    joined_state = jnp.where(vacant, high_state, low_state + jnp.where(same_block, high_state, 0.0))
    joined_sum = jnp.where(vacant, high_sum, low_sum + jnp.where(same_block, high_sum, 0.0))
    return (joined_id, joined_state, joined_sum)


def conv_taps(rows, weight, frame_count):
    result = jnp.einsum(
        "yfxc,co->yfxo", rows[:, 2 : 2 + frame_count], weight[0], preferred_element_type=jnp.float32
    )
    result = result + jnp.einsum(
        "yfxc,co->yfxo", rows[:, 1 : 1 + frame_count], weight[1], preferred_element_type=jnp.float32
    )
    result = result + jnp.einsum(
        "yfxc,co->yfxo", rows[:, 0:frame_count], weight[2], preferred_element_type=jnp.float32
    )
    return result


def per_device(
    queries,
    key_vectors,
    value_vectors,
    frame_index,
    height_index,
    width_index,
    frame_block,
    conv_weight,
    conv_bias,
):
    frame_count, height_count, width_count, channel_count = queries.shape
    head_count = channel_count // HD
    split_shape = (frame_count, height_count, width_count, head_count, HD)
    query_pos = jax.nn.relu(queries.astype(jnp.float32)).reshape(split_shape)
    key_pos = jax.nn.relu(key_vectors.astype(jnp.float32)).reshape(split_shape)
    value_rows = value_vectors.astype(jnp.float32).reshape(split_shape)
    query_rot = rotate(query_pos, frame_index, height_index, width_index)
    key_rot = rotate(key_pos, frame_index, height_index, width_index)
    frame_states = jnp.einsum("fyxhd,fyxhe->fhde", key_rot, value_rows, precision=HIGHEST)
    frame_sums = jnp.sum(key_pos, axis=(1, 2))
    block_float = frame_block.astype(jnp.float32)
    allowed = (frame_block[None, :] <= frame_block[:, None]).astype(jnp.float32)
    device_state = jnp.sum(frame_states, axis=0)
    device_sum = jnp.sum(frame_sums, axis=0)
    leading = (frame_block == frame_block[0]).astype(jnp.float32)
    lead_state = jnp.einsum("f,fhde->hde", leading, frame_states, precision=HIGHEST)
    lead_sum = jnp.einsum("f,fhd->hd", leading, frame_sums, precision=HIGHEST)
    lead_id = block_float[0]
    before_state, before_sum = prefix(
        (device_state, device_sum),
        "frame",
        add_pair,
        (jnp.zeros_like(device_state), jnp.zeros_like(device_sum)),
        False,
    )
    tail_id, tail_state, tail_sum = prefix(
        (lead_id, lead_state, lead_sum),
        "frame",
        join_tails,
        (jnp.full((), -1.0, jnp.float32), jnp.zeros_like(lead_state), jnp.zeros_like(lead_sum)),
        True,
    )
    matching = (block_float == tail_id).astype(jnp.float32)
    tail_states = matching[:, None, None, None] * tail_state[None]
    tail_sums = matching[:, None, None] * tail_sum[None]
    states = (
        before_state[None]
        + jnp.einsum("tf,fhde->thde", allowed, frame_states, precision=HIGHEST)
        + tail_states
    )
    key_totals = (
        before_sum[None]
        + jnp.einsum("tf,fhd->thd", allowed, frame_sums, precision=HIGHEST)
        + tail_sums
    )
    numerator = jnp.einsum("tyxhd,thde->tyxhe", query_rot, states, precision=HIGHEST)
    denominator = jnp.einsum("tyxhd,thd->tyxh", query_pos, key_totals, precision=HIGHEST) + EPSILON
    attended = (
        (numerator / denominator[..., None])
        .astype(jnp.bfloat16)
        .reshape(frame_count, height_count, width_count, channel_count)
    )
    ordered = jnp.transpose(attended, (1, 0, 2, 3))
    regrouped = lax.all_to_all(ordered, "head", split_axis=0, concat_axis=3, tiled=True)
    previous = shifted(regrouped, "frame", 1)
    extended = jnp.concatenate([previous, regrouped], axis=1)
    summed = conv_taps(
        extended, lax.all_gather(conv_weight, "head", axis=1, tiled=True), frame_count
    )
    return jax.nn.silu(summed + conv_bias).astype(jnp.bfloat16)


def solution(mesh):
    placed = (
        P("frame", None, None, "head"),
        P("frame", None, None, "head"),
        P("frame", None, None, "head"),
        P("frame"),
        P(),
        P(),
        P("frame"),
        P(None, "head", None),
        P(),
    )
    return jax.shard_map(
        per_device,
        mesh=mesh,
        in_specs=placed,
        out_specs=P("head", "frame", None, None),
        check_vma=False,
    )
```

profile of v0, /device:TPU:0, one launch (start us, length us, event | category | flops | bytes accessed | tf_op | source)
XLA Modules:
  0.0 197.5 jit_solution(477195029915813383)
XLA Ops:
  6.5 0.7 all-gather.6.cloned.1.call-update
  7.9 0.7 slice_dynamic-update-slice_fusion
  8.6 23.1 %all-reduce = f32[8]{0:T(128)S(1)} all-reduce(f32[8]{0:T(128)S(1)} %slice_dynamic-update-slice_fusion), channel_id=1, replica_groups=mesh['frame'=8,'head'=4] {'frame'}, use_global_device_ids=true, to_apply=%add | all-reduce | flops 8 | bytes 64
  33.9 0.6 fusion.38
  34.5 2.2 %fusion.37 = (f32[2,8,32,2,20]{4,3,2,1,0:T(2,128)S(1)}, f32[2,8,32,2,20]{4,3,2,1,0:T(2,128)S(1)}, f32[2,8,32,2,20]{4,3,2,1,0:T(2,128)S(1)}, f32[2,8,32,2,20]{4,3,2,1,0:T(2,128)S(1)}) fusion(f32[2,8,32,2,112]{4,3,2,1,0:T(2,128)S(1)} %reshape.194), kind=kLoop, calls=%fused_computation.78 | loop fusion | bytes 655360 | tf_op jit(solution)/shard_map/slice | solution.py:45
  36.7 1.6 multiply_add_fusion.5
  38.3 2.1 %multiply_add_fusion.3 = (f32[2,8,32,2,20]{4,2,1,3,0:T(8,128)S(1)}, f32[2,8,32,2,20]{4,2,1,3,0:T(8,128)S(1)}, f32[2,8,32,2,20]{4,2,1,3,0:T(8,128)S(1)}, f32[2,8,...) fusion(f32[2,8,32,2,20]{4,3,2,1,0:T(2,128)S(1)} %get-tuple-elem, ...), kind=kLoop, calls=%fused_computation.30 | loop fusion | flops 491520 | bytes 1317120 | tf_op jit(solution)/shard_map/add | solution.py:50
  40.5 2.1 %concatenate.9 = f32[2,8,32,2,112]{4,2,1,3,0:T(8,128)S(1)} concatenate(f32[2,8,32,2,16]{4,2,1,3,0:T(8,128)} %get-tuple-element.344, f32[2,8,32,2,16]{4,2,1,3,0:T(8,128)} %get-tuple-element.343, f32[2,8,32,2,20]{4,2,1,3,0:T(8,128)} %get-tuple-element.364, f32[2,8,32,2,20]{4,2,1,3,0:T(8,128)} %get-tuple-element.365, f32[2,8,32,2,20]{4,2,1,3,0:T(8,128)S(1)} %get-tuple-element.340, ...), dimensions={4} | concatenate | bytes 917504 | tf_op jit(solution)/shard_map/concatenate | solution.py:60
  42.6 0.6 fusion.39
  43.2 0.7 fusion.17
  43.9 32.8 %all-gather.1 = f32[16,112,112]{2,1,0:T(8,128)S(1)} all-gather(f32[2,112,112]{2,1,0:T(8,128)S(1)} %bitcast.116), channel_id=3, replica_groups=mesh['frame'=8,'head'=4] {'frame'}, dimensions={0}, use_global_device_ids=true | all-gather | bytes 903168 | tf_op jit(solution)/shard_map/all_gather | solution.py:15
  77.0 16.8 %all-gather.3 = f32[8,2,112]{2,1,0:T(2,128)S(1)} all-gather(f32[1,2,112]{2,1,0:T(2,128)S(1)} %bitcast.118), channel_id=4, replica_groups=mesh['frame'=8,'head'=4] {'frame'}, dimensions={0}, use_global_device_ids=true | all-gather | bytes 8064 | tf_op jit(solution)/shard_map/all_gather | solution.py:15
  93.9 2.2 %concatenate.10 = f32[2,8,32,2,112]{4,2,1,3,0:T(8,128)S(1)} concatenate(f32[2,8,32,2,16]{4,2,1,3,0:T(8,128)} %get-tuple-element.366, f32[2,8,32,2,16]{4,2,1,3,0:T(8,128)} %get-tuple-element.367, f32[2,8,32,2,20]{4,2,1,3,0:T(8,128)} %get-tuple-element.361, f32[2,8,32,2,20]{4,2,1,3,0:T(8,128)S(1)} %get-tuple-element.360, f32[2,8,32,2,20]{4,2,1,3,0:T(8,128)} %get-tuple-element.362, ...), dimensions={4} | concatenate | bytes 917504 | tf_op jit(solution)/shard_map/concatenate | solution.py:60
  96.1 17.9 %all_gather.33 = f32[8,2,112]{2,1,0:T(2,128)S(1)} all-gather(f32[1,2,112]{2,1,0:T(2,128)S(1)} %all_gather.32), channel_id=1, replica_groups=mesh['frame'=8,'head'=4] {'frame'}, dimensions={0}, use_global_device_ids=true | all-gather | bytes 8064 | tf_op jit(solution)/shard_map/all_gather | solution.py:15
  114.0 17.8 %while.35 = (s32[]{:T(128)}, f32[]{:T(128)}, f32[2,112,112]{2,1,0:T(8,128)S(1)}, f32[2,112]{1,0:T(2,128)S(1)}, s32[]{:T(128)}, /*index=5*/f32[8]{0:T(128)S(1)}, ...) while((s32[]{:T(128)}, f32[]{:T(128)}, ...), condition=%wide.region_6.7_spmd.clone, body=%wide.region_5.6_spmd.clone.sunk | while | flops 126568 | bytes 303943 | solution.py:27
  131.8 32.2 %all-gather = f32[16,112,112]{2,1,0:T(8,128)S(1)} all-gather(f32[2,112,112]{2,1,0:T(8,128)S(1)} %get-tuple-element.374), channel_id=2, replica_groups=mesh['frame'=8,'head'=4] {'frame'}, dimensions={0}, use_global_device_ids=true | all-gather | bytes 903168 | tf_op jit(solution)/shard_map/all_gather | solution.py:15
  164.7 2.1 %fusion.20 = f32[2,2,1,8,32]{4,2,3,1,0:T(1,128)S(1)} fusion(f32[2,2,112,1,1]{2,0,1,3,4:T(2,128)S(1)} %fusion.8, f32[2,8,32,2,112]{4,3,2,1,0:T(2,128)S(1)} %reshape.196), kind=kOutput, calls=%fused_computation.55 | convolution fusion | flops 1376256 | bytes 464640 | tf_op jit(solution)/shard_map/tyxhd,thd->tyxh/dot_general | solution.py:155
  166.8 0.7 fusion.6
  168.8 8.4 %all_to_all.18 = bf16[8,2,32,224]{3,2,1,0:T(8,128)(2,1)S(1)} all-to-all(bf16[8,2,32,224]{3,2,1,0:T(8,128)(2,1)S(1)} %copy.67), channel_id=1, replica_groups=mesh['frame'=8,'head'=4] {'head'}, dimensions={0} | all-to-all | bytes 458752 | tf_op jit(solution)/shard_map/all_to_all | solution.py:162
  177.7 1.3 collective-permute-start
  179.0 2.9 %fusion.2 = f32[2,2,32,2240]{3,2,1,0:T(8,128)S(1)} fusion(bf16[2,2,32,896]{3,2,1,0:T(8,128)(2,1)S(1)} %all_to_all.16, bf16[3,896,2240]{2,1,0:T(8,128)(2,1)} %all-gather.6.cloned.1.call-done), kind=kOutput, calls=%fused_computation.11 | convolution fusion | flops 513802240 | bytes 5505024 | tf_op jit(solution)/shard_map/yfxc,co->yfxo/dot_general | solution.py:86
  182.0 1.7 collective-permute-done
  183.7 2.9 %fusion = f32[2,2,32,2240]{3,2,1,0:T(8,128)S(1)} fusion(bf16[2,2,32,896]{3,2,1,0:T(8,128)(2,1)S(1)} %collective-permute-done, bf16[3,896,2240]{2,1,0:T(8,128)(2,1)} %all-gather.6.cloned.1.call-done), kind=kOutput, calls=%fused_computation.7 | convolution fusion | flops 513802240 | bytes 5505024 | tf_op jit(solution)/shard_map/yfxc,co->yfxo/dot_general | solution.py:92
  186.7 4.0 %multiply_convert_fusion = bf16[2,2,32,2240]{3,2,1,0:T(8,128)(2,1)} fusion(f32[2,2,32,2240]{3,2,1,0:T(8,128)S(1)} %fusion, f32[2,2,32,2240]{3,2,1,0:T(8,128)S(1)} %fusion.2, bf16[3,896,2240]{2,1,0:T(8,128)(2,1)} %all-gather.6.cloned.1.call-done, f32[2240]{0:T(1024)S(1)} %copy-done.5, bf16[2,2,32,896]{3,2,1,0:T(8,128)(2,1)S(1)} %all_to_all.16, ...), kind=kOutput, calls=%fused_computation.15 | convolution fusion | flops 517013504 | bytes 7463680 | tf_op jit(solution)/shard_map/yfxc,co->yfxo/dot_general | solution.py:89
  (97 shorter events, 10.4 us)
Async XLA Ops:
  6.5 0.8 copy-start.10
  6.5 0.7 copy-start.9
  6.5 25.2 %copy-start.1 = (bf16[2,8,32,224]{3,2,1,0:T(8,128)(2,1)S(1)}, bf16[2,8,32,224]{3,2,1,0:T(8,128)(2,1)}, u32[]{:S(2)}) copy-start(bf16[2,8,32,224]{3,2,1,0:T(8,128)(2,1)} %param.14) | copy-start | bytes 688132
  6.5 172.5 %all-gather.6.cloned.1.call-start = ((), (), s32[]{:S(2)}) async-start(), calls=%async_computation.1 | async-start | bytes 15482880 | tf_op jit(solution)/shard_map/all_gather | solution.py:166
  7.3 25.0 %copy-start = (bf16[2,8,32,224]{3,2,1,0:T(8,128)(2,1)S(1)}, bf16[2,8,32,224]{3,2,1,0:T(8,128)(2,1)}, u32[]{:S(2)}) copy-start(bf16[2,8,32,224]{3,2,1,0:T(8,128)(2,1)} %param.13) | copy-start | bytes 688132
  32.3 0.7 copy-start.6
  32.3 0.7 copy-start.7
  32.3 0.7 copy-start.8
  32.3 1.0 copy-start.2
  43.2 33.5 %copy-start.3 = (f32[2,2,112,112]{3,2,1,0:T(8,128)}, f32[2,2,112,112]{3,2,1,0:T(8,128)S(1)}, u32[]{:S(2)}) copy-start(f32[2,2,112,112]{3,2,1,0:T(8,128)S(1)} %get-tuple-element.375) | copy-start | bytes 602116
  164.0 2.9 %copy-start.4 = (f32[2,2,112,112]{3,2,1,0:T(8,128)S(1)}, f32[2,2,112,112]{3,2,1,0:T(8,128)}, u32[]{:S(2)}) copy-start(f32[2,2,112,112]{3,2,1,0:T(8,128)} %copy-done.3) | copy-start | bytes 602116
  177.7 6.1 %collective-permute-start = (bf16[2,2,32,896]{3,2,1,0:T(8,128)(2,1)S(1)}, bf16[2,2,32,896]{3,2,1,0:T(8,128)(2,1)S(1)}, u32[]{:S(2)}, u32[]{:S(2)}) collective-permute-start(bf16[2,2,32,896]{3,2,1,0:T(8,128)(2,1)S(1)} %all_to_all.16), channel_id=1, source_target_pairs={{0,4},{4,8},{8,12},{12,16},{16,20},{20,24},{24,28},{1,5},{5,9},{9,... | collective-permute-start | bytes 688136 | tf_op jit(solution)/shard_map/ppermute | solution.py:33
  182.0 4.7 %copy-start.5 = (f32[2240]{0:T(1024)S(1)}, f32[2240]{0:T(1024)}, u32[]{:S(2)}) copy-start(f32[2240]{0:T(1024)} %param.21) | copy-start | bytes 26884
Sparse Core Ops, SparseCore 0:
  8.9 83.6 all-gather.5
where the time goes:
time: 198 us
  blocking collectives  131 us (66%)
  local copies, waits for them, and re-layouts  15.2 us (8%)
  matrix products  14.9 us (8%)
  between operations  13.8 us (7%)
  loops' own time  13.4 us (7%)
  other arithmetic  5.27 us (3%)
  waiting for transfers between devices  2.48 us (1%)
    all_gather x4, blocking collectives, prefix(): pieces = jax.tree.map(lambda part: lax.all_gather(part, axis), value)  99.6 us
    unnamed x1, blocking collectives  23.1 us
    another operation x2, loops' own time, prefix(): return lax.fori_loop(0, count - 1, step, so_far)  13.4 us
    all_to_all x1, blocking collectives, per_device(): lax.all_to_all(ordered, 'head', split_axis=0, concat_axis=3, tiled=True)  8.42 us
    concatenate x2, local copies, waits for them, and re-layouts, rotate(): jnp.concatenate([spin_part(values[..., :first_size], frame_pos, 0), spin_...  4.25 us
    dynamic_slice x7, local copies, waits for them, and re-layouts, step(): longer = join(so_far, jax.tree.map(lambda part: part[position], pieces))  4.14 us
    dot_general x1, matrix products, conv_taps(): jnp.einsum('yfxc,co->yfxo', rows[:, 1:1 + frame_count], weight[1], prefer...  3.98 us
  transfers between devices with their start and end apart: 2, of which 1 were waited for; matrix products, arithmetic and copies ran while one was open for 14% of the time, Pallas kernels for 0%

commit v1 on v0

v1 whole, which is shorter than its diff:
```python
import functools

import jax
import jax.numpy as jnp
import numpy as np
from jax import lax
from jax.experimental import pallas as pl
from jax.experimental.pallas import tpu as pltpu
from jax.sharding import PartitionSpec as P

HD = 112
PAD = 128
EPSILON = 1e-06
BLOCK_MOST = 6
COLUMNS = 512
F32 = jnp.float32
BF16 = jnp.bfloat16


def sections():
    side = HD * 5 // 14 // 2 * 2
    first = HD - 2 * side
    return ((0, first), (first, side), (first + side, side))


def tables(heads):
    spread = np.zeros((heads * HD, heads * PAD), np.float32)
    swap = np.zeros((heads * HD, heads * PAD), np.float32)
    freq = np.zeros((8, heads * PAD), np.float32)
    for h in range(heads):
        for j in range(HD):
            spread[h * HD + j, h * PAD + j] = 1.0
        for s, (start, n) in enumerate(sections()):
            half = n // 2
            for j in range(half):
                a, b = start + j, start + half + j
                swap[h * HD + b, h * PAD + a] = -1.0
                swap[h * HD + a, h * PAD + b] = 1.0
                for d in (a, b):
                    freq[s, h * PAD + d] = 10000.0 ** (-2.0 * j / n)
                    freq[3 + s, h * PAD + d] = 1.0
    return spread, swap, freq


def mm(a, b):
    return jnp.dot(a, b, preferred_element_type=F32)


def mm_t(a, b):
    return lax.dot_general(a, b, (((0,), (0,)), ((), ())), preferred_element_type=F32)


def split(a):
    high = a.astype(BF16)
    return high, (a - high.astype(F32)).astype(BF16)


def kernel(
    cfg, fb_ref, q_ref, k_ref, v_ref, pos_ref, freq_ref, spread_ref, swap_ref, gather_ref, w_ref, bias_ref, out_ref,
    w_buf, qh, time_own, time_prev, msg_t, msg_l, recv_t, recv_l, recv_p, state, att, att_x, *rest,
):
    F, Y, heads, HG, W, chunks = cfg
    n_chunk = len(chunks)
    part_send, part_recv, part_own = rest[:n_chunk], rest[n_chunk : 2 * n_chunk], rest[2 * n_chunk : 3 * n_chunk]
    (w_sem, w_send, w_recv, halo_send, halo_recv, t_send, t_recv, l_send, l_recv, p_send, p_recv,
     x_send, x_recv, c_send, c_recv) = rest[3 * n_chunk :]
    FC = 2
    H = 2 * Y
    TF = HG * W
    RD = HG // H
    TD = RD * W
    reach = min(F - 1, -(-(BLOCK_MOST - 1) // FC))
    f = lax.axis_index("frame")
    h = lax.axis_index("head")
    y, c = h // 2, h % 2
    mate = 2 * y + (1 - c)

    barrier = pltpu.get_barrier_semaphore()
    for k in range(1, F):
        pl.semaphore_signal(barrier, inc=1, device_id=(lax.rem(f + k, F), h), device_id_type=pl.DeviceIdType.MESH)
    pl.semaphore_signal(barrier, inc=1, device_id=(f, mate), device_id_type=pl.DeviceIdType.MESH)
    for j in range(1, Y):
        pl.semaphore_signal(
            barrier, inc=1, device_id=(f, 2 * lax.rem(y + j, Y) + c), device_id_type=pl.DeviceIdType.MESH
        )

    def remote(src, dst, send, recv, frame, head):
        return pltpu.make_async_remote_copy(
            src_ref=src, dst_ref=dst, send_sem=send, recv_sem=recv,
            device_id=(frame, head), device_id_type=pl.DeviceIdType.MESH,
        )

    w_local = pltpu.make_async_copy(w_ref, w_buf.at[0], w_sem)
    w_local.start()

    width = pos_ref[0:W, :]
    height = pos_ref[W : W + HG, :]
    times = pos_ref[W + HG : W + HG + 8, :]
    freq = freq_ref[...]
    t_ang = times * freq[0:1]
    time_own[0:8, :] = jnp.cos(t_ang) * freq[3:4]
    time_own[8:16, :] = jnp.sin(t_ang)
    h_ang = height * freq[1:2]
    w_ang = width * freq[2:3]
    lanes = heads * PAD
    cos_hw = (
        (jnp.cos(h_ang) * freq[4:5]).reshape(HG, 1, lanes) + (jnp.cos(w_ang) * freq[5:6]).reshape(1, W, lanes)
    ).reshape(TF, lanes)
    sin_hw = (jnp.sin(h_ang).reshape(HG, 1, lanes) + jnp.sin(w_ang).reshape(1, W, lanes)).reshape(TF, lanes)

    pl.semaphore_wait(barrier, (F - 1) + 1 + (Y - 1))

    w_far = remote(w_ref, w_buf.at[1], w_send, w_recv, f, mate)
    w_far.start()
    nxt = lax.rem(f + 1, F)
    q_copy = remote(q_ref, qh, halo_send.at[0], halo_recv.at[0], nxt, h)
    t_copy = remote(time_own, time_prev, halo_send.at[1], halo_recv.at[1], nxt, h)

    @pl.when(f < F - 1)
    def _():
        q_copy.start()
        t_copy.start()

    @pl.when(f == 0)
    def _():
        qh[...] = jnp.zeros_like(qh)
        time_prev[...] = jnp.zeros_like(time_prev)
        recv_t[0] = jnp.zeros_like(recv_t[0])
        recv_p[...] = jnp.zeros_like(recv_p)

    spread = spread_ref[...]
    swap = swap_ref[...]

    def rotated(rows, cos_t, sin_t):
        positive = jnp.maximum(rows, jnp.zeros_like(rows))
        plain = mm(positive, spread)
        turned = mm(positive, swap)
        return plain.astype(BF16), plain * (cos_hw + cos_t) + turned * (sin_hw + sin_t)

    lane = lax.broadcasted_iota(jnp.int32, (TF, PAD), 1)
    ones = jnp.where(lane >= HD, 1.0, 0.0).astype(BF16)
    frames = []
    for t in range(FC):
        rows = slice(t * TF, (t + 1) * TF)
        k_pos, k_rot = rotated(k_ref[rows, :], time_own[t : t + 1, :], time_own[8 + t : 9 + t, :])
        k_hi, k_lo = split(k_rot)
        value = mm(v_ref[rows, :], spread).astype(BF16)
        per_head = []
        for g in range(heads):
            cut = slice(g * PAD, (g + 1) * PAD)
            per_head.append(
                mm_t(k_hi[:, cut], value[:, cut]) + mm_t(k_lo[:, cut], value[:, cut]) + mm_t(k_pos[:, cut], ones)
            )
        frames.append(jnp.concatenate(per_head, axis=0))
    id0 = fb_ref[0].astype(F32)
    id1 = fb_ref[1].astype(F32)
    own_t = frames[0] + frames[1]
    own_l = frames[0] + jnp.where(id0 == id1, 1.0, 0.0) * frames[1]
    row = lax.broadcasted_iota(jnp.int32, own_t.shape, 0)
    msg_t[...] = own_t.astype(BF16)
    msg_l[...] = jnp.where(row == HD, id0, jnp.where(row == HD + 1, id1, own_l)).astype(BF16)

    t_copies = {}
    l_copies = {}
    for k in range(1, F):
        t_copies[k] = remote(
            msg_t, recv_t.at[k - 1], t_send.at[k - 1], t_recv.at[k - 1], lax.rem(f + k, F), h
        )
    for k in range(1, reach + 1):
        l_copies[k] = remote(
            msg_l, recv_l.at[k - 1], l_send.at[k - 1], l_recv.at[k - 1], lax.rem(f - k + F, F), h
        )
    p_copy = remote(msg_l, recv_p, p_send, p_recv, nxt, h)
    for k in range(F - 1, 0, -1):

        @pl.when(f + k < F)
        def _(k=k):
            t_copies[k].start()

    @pl.when(f < F - 1)
    def _():
        p_copy.start()

    for k in range(reach, 0, -1):

        @pl.when(f >= k)
        def _(k=k):
            l_copies[k].start()

    q_parts = [None, None]
    for t in range(FC):
        rows = slice(t * TF, (t + 1) * TF)
        q_parts.append(rotated(q_ref[rows, :], time_own[t : t + 1, :], time_own[8 + t : 9 + t, :]))

    @pl.when(f > 0)
    def _():
        q_copy.wait_recv()
        t_copy.wait_recv()

    for t in range(FC):
        rows = slice(t * TF, (t + 1) * TF)
        q_parts[t] = rotated(qh[rows, :], time_prev[t : t + 1, :], time_prev[8 + t : 9 + t, :])

    state[2] = own_l
    state[3] = own_t

    @pl.when(f > 0)
    def _():
        p_copy.wait_recv()
        t_copies[1].wait_recv()

    lead_prev = recv_p[...].astype(F32)
    state[0] = lead_prev
    all_prev = recv_t[0].astype(F32)
    state[1] = all_prev
    state[2] += all_prev
    state[3] += all_prev
    ids = [lead_prev[HD : HD + 1], lead_prev[HD + 1 : HD + 2], id0, id1]

    def add_tail(i, other, lead):
        state[i] += jnp.where(other == ids[i], 1.0, 0.0) * lead

    for i in range(2):
        add_tail(i, id0, own_l)
    for k in range(1, reach + 1):

        @pl.when(f + k < F)
        def _(k=k):
            l_copies[k].wait_recv()
            lead = recv_l[k - 1].astype(F32)
            for i in range(4):
                add_tail(i, lead[HD : HD + 1], lead)

    for k in range(2, F):

        @pl.when(f >= k)
        def _(k=k):
            t_copies[k].wait_recv()
            piece = recv_t[k - 1].astype(F32)
            for i in range(4):
                state[i] += piece

    for t in range(2 + FC):
        q_pos, q_rot = q_parts[t]
        q_hi, q_lo = split(q_rot)
        full = state[t]
        merged = []
        for g in range(heads):
            cut = slice(g * PAD, (g + 1) * PAD)
            block = full[cut, :]
            s_hi, s_lo = split(block)
            total_hi, total_lo = split(jnp.broadcast_to(block[:, HD : HD + 1], (PAD, PAD)))
            numerator = mm(q_hi[:, cut], s_hi) + mm(q_lo[:, cut], s_hi) + mm(q_hi[:, cut], s_lo)
            denominator = mm(q_pos[:, cut], total_hi) + mm(q_pos[:, cut], total_lo) + EPSILON
            merged.append((numerator / denominator).astype(BF16))
        tight = mm(jnp.concatenate(merged, axis=1), gather_ref[...]).astype(BF16)
        for g in range(H):
            att[g, t] = tight[g * TD : (g + 1) * TD]

    x_copies = []
    for j in range(Y):
        x_copies.append(remote(att.at[2 * j + 1 - c], att_x.at[j], x_send.at[j], x_recv.at[j], f, mate))
        x_copies[-1].start()
    w_local.wait()
    w_far.wait_recv()
    for copy in x_copies:
        copy.wait_recv()

    starts = np.cumsum([0] + list(chunks))

    def conv(j, n):
        cols = slice(int(starts[n]), int(starts[n + 1]))
        total = None
        for tap in range(3):
            for side in range(2):
                source = att.at[2 * j + c] if side == 0 else att_x.at[j]
                rows = source[2 - tap : 2 - tap + FC].reshape(FC * TD, heads * HD)
                term = mm(rows, w_buf[side, tap, :, cols])
                total = term if total is None else total + term
        return total

    c_copies = []
    for j in range(1, Y):
        target = lax.rem(y + j, Y)
        for n in range(n_chunk):
            part_send[n][j - 1] = conv(target, n).astype(BF16)
            slot = (j - 1) * n_chunk + n
            copy = remote(
                part_send[n].at[j - 1], part_recv[n].at[j - 1], c_send.at[slot], c_recv.at[slot], f, 2 * target + c
            )
            copy.start()
            c_copies.append(copy)
    for n in range(n_chunk):
        part_own[n][...] = conv(y, n)
    for n in range(n_chunk):
        cols = slice(int(starts[n]), int(starts[n + 1]))
        total = part_own[n][...]
        for j in range(1, Y):
            c_copies[(j - 1) * n_chunk + n].wait_recv()
            total = total + part_recv[n][j - 1].astype(F32)
        total = total + bias_ref[:, cols]
        result = (total / (1.0 + jnp.exp(-total))).astype(BF16)
        for t in range(FC):
            for r in range(RD):
                start = t * TD + r * W
                out_ref[r, t, :, cols] = result[start : start + W]

    w_far.wait_send()
    for copy in x_copies + c_copies:
        copy.wait_send()

    @pl.when(f < F - 1)
    def _():
        q_copy.wait_send()
        t_copy.wait_send()
        p_copy.wait_send()

    for k in range(1, F):

        @pl.when(f + k < F)
        def _(k=k):
            t_copies[k].wait_send()

    for k in range(1, reach + 1):

        @pl.when(f >= k)
        def _(k=k):
            l_copies[k].wait_send()


def per_device(F, H, queries, key_vectors, value_vectors, frame_index, height_index, width_index, frame_block,
               conv_weight, conv_bias):
    FC, HG, W, C = queries.shape
    heads = C // HD
    assert FC == 2 and H % 2 == 0
    Y = H // 2
    T, TF, RD = FC * HG * W, HG * W, HG // H
    TD = RD * W
    O = conv_weight.shape[-1]
    chunks = [COLUMNS] * (O // COLUMNS) + ([O % COLUMNS] if O % COLUMNS else [])
    spread, swap, freq = tables(heads)
    positions = jnp.concatenate(
        [width_index, height_index, frame_index, jnp.zeros((8 - FC,), jnp.int32)]
    ).astype(F32)[:, None]
    reach = min(F - 1, -(-(BLOCK_MOST - 1) // FC))
    lanes = heads * PAD
    vmem = pl.BlockSpec(memory_space=pltpu.VMEM)
    dma = pltpu.SemaphoreType.DMA
    return pl.pallas_call(
        functools.partial(kernel, (F, Y, heads, HG, W, tuple(chunks))),
        out_shape=jax.ShapeDtypeStruct((RD, FC, W, O), BF16),
        in_specs=[pl.BlockSpec(memory_space=pltpu.SMEM)] + [vmem] * 8 + [pl.BlockSpec(memory_space=pl.ANY), vmem],
        out_specs=vmem,
        scratch_shapes=[
            pltpu.VMEM((2,) + conv_weight.shape, BF16),
            pltpu.VMEM((T, C), BF16),
            pltpu.VMEM((16, lanes), F32),
            pltpu.VMEM((16, lanes), F32),
            pltpu.VMEM((lanes, PAD), BF16),
            pltpu.VMEM((lanes, PAD), BF16),
            pltpu.VMEM((max(F - 1, 1), lanes, PAD), BF16),
            pltpu.VMEM((max(reach, 1), lanes, PAD), BF16),
            pltpu.VMEM((lanes, PAD), BF16),
            pltpu.VMEM((4, lanes, PAD), F32),
            pltpu.VMEM((H, 2 + FC, TD, C), BF16),
            pltpu.VMEM((Y, 2 + FC, TD, C), BF16),
        ]
        + [pltpu.VMEM((max(Y - 1, 1), FC * TD, n), BF16) for n in chunks]
        + [pltpu.VMEM((max(Y - 1, 1), FC * TD, n), BF16) for n in chunks]
        + [pltpu.VMEM((FC * TD, n), F32) for n in chunks]
        + [
            dma, dma, dma, dma((2,)), dma((2,)),
            dma((max(F - 1, 1),)), dma((max(F - 1, 1),)),
            dma((max(reach, 1),)), dma((max(reach, 1),)),
            dma, dma,
            dma((Y,)), dma((Y,)),
            dma((max(Y - 1, 1) * len(chunks),)), dma((max(Y - 1, 1) * len(chunks),)),
        ],
        compiler_params=pltpu.CompilerParams(
            collective_id=0, has_side_effects=True, vmem_limit_bytes=48 * 1024 * 1024
        ),
        name="attend_conv",
    )(
        frame_block,
        queries.reshape(T, C),
        key_vectors.reshape(T, C),
        value_vectors.reshape(T, C),
        positions,
        jnp.asarray(freq),
        jnp.asarray(spread, BF16),
        jnp.asarray(swap, BF16),
        jnp.asarray(spread.T, BF16),
        conv_weight,
        conv_bias[None, :],
    )


def solution(mesh):
    placed = (
        P("frame", None, None, "head"),
        P("frame", None, None, "head"),
        P("frame", None, None, "head"),
        P("frame"),
        P(),
        P(),
        P("frame"),
        P(None, "head", None),
        P(),
    )
    return jax.shard_map(
        functools.partial(per_device, mesh.shape["frame"], mesh.shape["head"]),
        mesh=mesh,
        in_specs=placed,
        out_specs=P("head", "frame", None, None),
        check_vma=False,
    )
```

time: 198 us -> 55.1 us (0.28)
  the two profiles are of different devices: /device:TPU:0 before, /device:TPU:17 now
where the time goes in v1:
time: 55.1 us; the launch traced here: 54.7 us
  Pallas kernels  43.5 us (79%)
  local copies, waits for them, and re-layouts  10.4 us (19%)
  other arithmetic  0.76 us (1%)
    pallas_call x1, Pallas kernels, per_device(): pl.pallas_call(functools.partial(kernel, (F, Y, heads, HG, W, tuple(chunk...  43.5 us
    unnamed x19, local copies, waits for them, and re-layouts  9.59 us

profile of v1, /device:TPU:17, one launch (start us, length us, event | category | flops | bytes accessed | tf_op | source)
XLA Modules:
  0.0 54.7 jit_solution(17497406163315419119)
XLA Ops:
  0.0 0.8 %fusion = f32[48,1]{0,1:T(1,128)S(1)} fusion(s32[6]{0:T(128)S(1)} %concatenate.21, s32[2,1]{0,1:T(1,128)} %bitcast.13, s32[8,1]{0,1:T(1,128)} %bitcast.14, s32[32,1]{0,1:T(1,128)} %bitcast.15), kind=kLoop, calls=%fused_computation.1 | loop fusion | flops 192 | bytes 384 | tf_op jit(solution)/shard_map/convert_element_type | solution.py:344
  0.8 0.7 %broadcast_in_dim.4.bias_ref = f32[1,2240]{1,0:T(1,128)S(1)} reshape(f32[2240]{0:T(1024)} %param.21) | data formatting | bytes 17920 | tf_op jit(solution)/shard_map/broadcast_in_dim | solution.py:394
  1.5 0.1 copy.18.pos_ref
  1.6 0.0 copy-start
  1.6 1.9 %copy-done = bf16[3,224,2240]{2,1,0:T(8,128)(2,1)S(1)} copy-done((bf16[3,224,2240]{2,1,0:T(8,128)(2,1)S(1)}, bf16[3,224,2240]{2,1,0:T(8,128)(2,1)}, u32[]{:S(2)}) %copy-start) | copy-done | bytes 3010584
  3.4 0.0 copy-start.1
  3.5 0.9 %copy-done.1 = bf16[2,8,32,224]{3,2,1,0:T(8,128)(2,1)S(1)} copy-done((bf16[2,8,32,224]{3,2,1,0:T(8,128)(2,1)S(1)}, bf16[2,8,32,224]{3,2,1,0:T(8,128)(2,1)}, u32[]{:S(2)}) %copy-start.1) | copy-done | bytes 229400
  4.4 0.0 copy-start.2
  4.4 0.9 %copy-done.2 = bf16[2,8,32,224]{3,2,1,0:T(8,128)(2,1)S(1)} copy-done((bf16[2,8,32,224]{3,2,1,0:T(8,128)(2,1)S(1)}, bf16[2,8,32,224]{3,2,1,0:T(8,128)(2,1)}, u32[]{:S(2)}) %copy-start.2) | copy-done | bytes 229400
  5.4 0.0 copy-start.3
  5.4 0.9 %copy-done.3 = bf16[2,8,32,224]{3,2,1,0:T(8,128)(2,1)S(1)} copy-done((bf16[2,8,32,224]{3,2,1,0:T(8,128)(2,1)S(1)}, bf16[2,8,32,224]{3,2,1,0:T(8,128)(2,1)}, u32[]{:S(2)}) %copy-start.3) | copy-done | bytes 229400
  6.3 0.0 copy-start.4
  6.3 0.9 %copy-done.4 = bf16[256,224]{1,0:T(8,128)(2,1)S(1)} copy-done((bf16[256,224]{1,0:T(8,128)(2,1)S(1)}, bf16[256,224]{1,0:T(8,128)(2,1)}, u32[]{:S(2)}) %copy-start.4) | copy-done | bytes 114712
  7.2 0.0 copy-start.5
  7.2 0.9 %copy-done.5 = bf16[224,256]{1,0:T(8,128)(2,1)S(1)} copy-done((bf16[224,256]{1,0:T(8,128)(2,1)S(1)}, bf16[224,256]{1,0:T(8,128)(2,1)}, u32[]{:S(2)}) %copy-start.5) | copy-done | bytes 114712
  8.1 0.0 copy-start.6
  8.1 0.9 %copy-done.6 = bf16[224,256]{1,0:T(8,128)(2,1)S(1)} copy-done((bf16[224,256]{1,0:T(8,128)(2,1)S(1)}, bf16[224,256]{1,0:T(8,128)(2,1)}, u32[]{:S(2)}) %copy-start.6) | copy-done | bytes 114712
  9.0 0.0 copy-start.7
  9.0 0.7 %copy-done.7 = f32[8,256]{1,0:T(8,128)S(1)} copy-done((f32[8,256]{1,0:T(8,128)S(1)}, f32[8,256]{1,0:T(8,128)}, u32[]{:S(2)}) %copy-start.7) | copy-done | bytes 8216
  9.7 0.0 copy-start.8
  9.7 0.7 %copy-done.8 = s32[2]{0:T(128)S(1)} copy-done((s32[2]{0:T(128)S(1)}, s32[2]{0:T(128)}, u32[]{:S(2)}) %copy-start.8) | copy-done | bytes 32
  10.4 43.5 %attend_conv.1 = bf16[2,2,32,2240]{3,2,1,0:T(8,128)(2,1)S(1)} custom-call(s32[2]{0:T(128)S(1)} %copy-done.8, bf16[512,224]{1,0:T(8,128)(2,1)S(1)} %bitcast.10, bf16[512,224]{1,0:T(8,128)(2,1)S(1)} %bitcast.11, bf16[512,224]{1,0:T(8,128)(2,1)S(1)} %bitcast.12, f32[48,1]{1,0:T(8,128)S(1)} %copy.18.pos_ref, f32[8,256]{1,0:T(8,128)S(1)} %copy-done.7, ...), custom_call_target="tpu_custom_call" | custom-call | tf_op jit(solution)/shard_map/attend_conv/pallas_call | solution.py:349
  53.9 0.8 %copy.20 = bf16[2,2,32,2240]{3,2,1,0:T(8,128)(2,1)} copy(bf16[2,2,32,2240]{3,2,1,0:T(8,128)(2,1)S(1)} %attend_conv.1) | data formatting | bytes 1146880
  (1 shorter events, 0.0 us)
Async XLA Ops:
  1.6 1.9 %copy-start = (bf16[3,224,2240]{2,1,0:T(8,128)(2,1)S(1)}, bf16[3,224,2240]{2,1,0:T(8,128)(2,1)}, u32[]{:S(2)}) copy-start(bf16[3,224,2240]{2,1,0:T(8,128)(2,1)} %w_ref.1) | copy-start | bytes 9031684
  3.4 0.9 %copy-start.1 = (bf16[2,8,32,224]{3,2,1,0:T(8,128)(2,1)S(1)}, bf16[2,8,32,224]{3,2,1,0:T(8,128)(2,1)}, u32[]{:S(2)}) copy-start(bf16[2,8,32,224]{3,2,1,0:T(8,128)(2,1)} %param.13) | copy-start | bytes 688132
  4.4 0.9 %copy-start.2 = (bf16[2,8,32,224]{3,2,1,0:T(8,128)(2,1)S(1)}, bf16[2,8,32,224]{3,2,1,0:T(8,128)(2,1)}, u32[]{:S(2)}) copy-start(bf16[2,8,32,224]{3,2,1,0:T(8,128)(2,1)} %param.14) | copy-start | bytes 688132
  5.4 0.9 %copy-start.3 = (bf16[2,8,32,224]{3,2,1,0:T(8,128)(2,1)S(1)}, bf16[2,8,32,224]{3,2,1,0:T(8,128)(2,1)}, u32[]{:S(2)}) copy-start(bf16[2,8,32,224]{3,2,1,0:T(8,128)(2,1)} %param.15) | copy-start | bytes 688132
  6.3 0.9 %copy-start.4 = (bf16[256,224]{1,0:T(8,128)(2,1)S(1)}, bf16[256,224]{1,0:T(8,128)(2,1)}, u32[]{:S(2)}) copy-start(bf16[256,224]{1,0:T(8,128)(2,1)} %constant.13.clone.gather_ref) | copy-start | bytes 344068
  7.2 0.9 %copy-start.5 = (bf16[224,256]{1,0:T(8,128)(2,1)S(1)}, bf16[224,256]{1,0:T(8,128)(2,1)}, u32[]{:S(2)}) copy-start(bf16[224,256]{1,0:T(8,128)(2,1)} %constant.12.clone.swap_ref) | copy-start | bytes 344068
  8.1 0.9 %copy-start.6 = (bf16[224,256]{1,0:T(8,128)(2,1)S(1)}, bf16[224,256]{1,0:T(8,128)(2,1)}, u32[]{:S(2)}) copy-start(bf16[224,256]{1,0:T(8,128)(2,1)} %constant.11.clone.spread_ref) | copy-start | bytes 344068
  9.0 0.7 %copy-start.7 = (f32[8,256]{1,0:T(8,128)S(1)}, f32[8,256]{1,0:T(8,128)}, u32[]{:S(2)}) copy-start(f32[8,256]{1,0:T(8,128)} %constant.10.clone.freq_ref) | copy-start | bytes 24580
  9.7 0.7 %copy-start.8 = (s32[2]{0:T(128)S(1)}, s32[2]{0:T(128)}, u32[]{:S(2)}) copy-start(s32[2]{0:T(128)} %fb_ref.1) | copy-start | bytes 28
